TPU v7x, 32 devices: a whole 2x2x4 slice. The times are simulated.
32 devices in a mesh: dp: 2 (over x), ctx: 4 (over z), tp: 4 (over y, core).
Axes of the slice: x: 2, y: 2, z: 4, core: 2. Of those that a mesh axis runs over, the one named last changes fastest.
Arguments:
- routed_experts: int32 [512, 8], P(('dp', 'ctx', 'tp')), may hold values from 0 to 15, all different within a row; in each aligned block of 16 rows (0 to 15, 16 to 31, ...) at most 9 rows name the same one
- route_gates: float32 [512, 8], P(('dp', 'ctx', 'tp')), may hold values from 0.03 to 0.4
- expert_hidden: bfloat16 [16, 2, 16, 9, 768], P(('ctx', 'tp'), 'dp'), may hold values from -6 to 6
- down_weight: bfloat16 [16, 768, 4096], P(('ctx', 'tp'), None, 'dp'), may hold values from -0.21875 to 0.21875
- output_grad: bfloat16 [512, 4096], P(('dp', 'ctx', 'tp')), may hold values from -1.5 to 1.5
Outputs:
- combined: bfloat16 [512, 4096], P(('dp', 'ctx', 'tp'))
- down_gradient: float32 [16, 768, 4096], P(('ctx', 'tp'), None, 'dp')
Inputs may be any that keep to these rules, and one draw needn't show every extreme that they name: `routed_experts`: each row names 8 different experts. Among the routes of one device's 16 tokens (aligned blocks of rows) no expert is named more than 9 times, and in every draw some block names some expert exactly 9 times.
All inputs are finite; a program needn't handle non-finite values.
Results may differ from a plain program's by a relative error of at most 0.0049.
Values may be sent and summed in bfloat16 or wider, within the bound.
A program may use at most 64 MiB of HBM per device.

v0:
```python
import jax
import jax.numpy as jnp
from jax import lax
from jax.sharding import PartitionSpec as P


def slot_ranks(flat_experts):
    count = flat_experts.shape[-1]
    same = flat_experts[..., :, None] == flat_experts[..., None, :]
    before = lax.broadcasted_iota(jnp.int32, (count, count), 1) < lax.broadcasted_iota(
        jnp.int32, (count, count), 0
    )
    return jnp.sum(jnp.logical_and(same, before), axis=-1)


def expert_move(buffer):
    return lax.all_to_all(buffer, ("ctx", "tp"), split_axis=0, concat_axis=0, tiled=True)


def body(routed_experts, route_gates, expert_hidden, down_weight, output_grad):
    replicas = lax.axis_size("dp")
    sources = lax.axis_size("ctx") * lax.axis_size("tp")
    tok_own, topk = routed_experts.shape
    routes = tok_own * topk
    capacity = expert_hidden.shape[3]
    width = output_grad.shape[1]
    column_part = width // replicas
    hidden_rows = expert_hidden[0]
    weight = down_weight[0]
    slot_count = sources * capacity
    expert_table, gate_table = (
        lax.all_gather(routed_experts.astype(jnp.float32), "dp", axis=0, tiled=True),
        lax.all_gather(route_gates, "dp", axis=0, tiled=True),
    )
    all_experts = expert_table.astype(jnp.int32).reshape(replicas, routes)
    all_gates = gate_table.reshape(replicas, tok_own, topk)
    grad_columns = lax.all_to_all(
        output_grad, "dp", split_axis=1, concat_axis=0, tiled=True
    ).reshape(replicas, tok_own, 1, column_part)
    ranks = slot_ranks(all_experts)
    target = all_experts * capacity + ranks
    placer = (
        lax.broadcasted_iota(jnp.int32, (1, slot_count, routes), 1) == target[:, None, :]
    ).astype(jnp.bfloat16)
    scaled = (
        (all_gates[:, :, :, None] * grad_columns.astype(jnp.float32))
        .reshape(replicas, routes, column_part)
        .astype(jnp.bfloat16)
    )
    outgoing = jnp.einsum("rpq,rqd->prd", placer, scaled, preferred_element_type=jnp.float32)
    outgoing = outgoing.astype(jnp.bfloat16).reshape(sources, capacity, replicas, column_part)
    grad_rows = expert_move(outgoing)
    piece = lax.all_gather(hidden_rows, "dp", axis=0, tiled=True)
    produced = jnp.einsum(
        "rsjf,fd->srjd", piece, weight, preferred_element_type=jnp.float32
    ).astype(jnp.bfloat16)
    outputs = produced
    gradient = jnp.einsum("rsjf,sjrd->fd", piece, grad_rows, preferred_element_type=jnp.float32)
    outputs, gradient = (outputs, gradient)
    returned = expert_move(outputs).reshape(sources * replicas * capacity, column_part)
    replica_index = lax.broadcasted_iota(jnp.int32, (replicas, routes), 0)
    position = all_experts * (replicas * capacity) + replica_index * capacity + ranks
    picked = (
        jnp.take(returned, position, axis=0)
        .astype(jnp.float32)
        .reshape(replicas, tok_own, topk, column_part)
    )
    partial_rows = jnp.sum(all_gates[:, :, :, None] * picked, axis=2).astype(jnp.bfloat16)
    combined = lax.all_to_all(partial_rows, "dp", split_axis=0, concat_axis=2, tiled=True)[0]
    return (combined, gradient[None])


def solution(mesh):
    in_specs = (
        P(("dp", "ctx", "tp"), None),
        P(("dp", "ctx", "tp"), None),
        P(("ctx", "tp"), "dp", None, None, None),
        P(("ctx", "tp"), None, "dp"),
        P(("dp", "ctx", "tp"), None),
    )
    out_specs = (P(("dp", "ctx", "tp"), None), P(("ctx", "tp"), None, "dp"))
    return jax.shard_map(body, mesh=mesh, in_specs=in_specs, out_specs=out_specs, check_vma=False)
```

profile of v0, /device:TPU:13, one launch (start us, length us, event | category | flops | bytes accessed | tf_op | source)
XLA Modules:
  0.0 120.6 jit_solution(13044856385677406198)
XLA Ops:
  0.6 1.7 %copy.76 = bf16[2,2,8,2048]{3,2,0,1:T(8,128)(2,1)} copy(bf16[2,2,8,2048]{3,2,1,0:T(8,128)(2,1)} %bitcast.61) | data formatting | bytes 262144 | tf_op jit(solution)/shard_map/all_to_all | solution.py:37
  2.4 3.4 %all-to-all-start.2 = ((bf16[16,2,2048]{2,0,1:T(8,128)(2,1)}), bf16[16,2,2048]{2,0,1:T(8,128)(2,1)S(1)}, u32[]{:S(2)}, u32[]{:S(2)}) async-start(bf16[16,2,2048]{2,0,1:T(8,128)(2,1)} %bitcast.57), calls=%async_computation.2 | async-start | bytes 262144 | tf_op jit(solution)/shard_map/all_to_all | solution.py:37
  5.8 8.0 %all-gather = bf16[2,1,16,9,768]{4,2,3,1,0:T(8,128)(2,1)S(1)} all-gather(bf16[1,1,16,9,768]{4,2,3,1,0:T(8,128)(2,1)} %param.7), channel_id=2, replica_groups=mesh['dp'=2,'ctx'=4,'tp'=4] {'dp'}, dimensions={0}, use_global_device_ids=true | all-gather | bytes 663552 | tf_op jit(solution)/shard_map/all_gather | solution.py:53
  13.8 0.8 copy-done.1
  14.5 1.1 fusion.6
  15.7 2.2 %copy.58 = bf16[16,2,9,2048]{3,1,2,0:T(2,128)(2,1)} copy(bf16[16,2,9,2048]{3,0,2,1:T(8,128)(2,1)S(1)} %fusion.6) | data formatting | bytes 2359296 | tf_op jit(solution)/shard_map/convert_element_type | solution.py:56
  17.9 7.3 %all-to-all-start = ((bf16[16,2,9,2048]{3,1,2,0:T(2,128)(2,1)}), bf16[16,2,9,2048]{3,1,2,0:T(2,128)(2,1)}, u32[]{:S(2)}, u32[]{:S(2)}) async-start(bf16[16,2,9,2048]{3,1,2,0:T(2,128)(2,1)} %copy.58), calls=%async_computation | async-start | bytes 2359296 | tf_op jit(solution)/shard_map/all_to_all | solution.py:17
  25.2 3.5 %all-gather.2 = f32[2,16,8]{1,2,0:T(8,128)S(1)} all-gather(f32[1,16,8]{1,2,0:T(8,128)S(1)} %convert_bitcast_fusion.1), channel_id=1, replica_groups=mesh['dp'=2,'ctx'=4,'tp'=4] {'dp'}, dimensions={0}, use_global_device_ids=true | all-gather | bytes 1536 | tf_op jit(solution)/shard_map/all_gather | solution.py:32
  28.8 3.2 %all-gather.1 = f32[2,16,8]{1,2,0:T(8,128)S(1)} all-gather(f32[1,16,8]{1,2,0:T(8,128)S(1)} %bitcast.63), channel_id=1, replica_groups=mesh['dp'=2,'ctx'=4,'tp'=4] {'dp'}, dimensions={0}, use_global_device_ids=true | all-gather | bytes 1536 | tf_op jit(solution)/shard_map/all_gather | solution.py:33
  32.1 0.6 mul.71
  32.7 0.1 mul.69
  32.8 0.1 reshape.120
  32.9 0.2 convert_reduce_fusion
  33.1 0.1 reduce_sum.23
  33.3 0.6 pad_clamp_fusion
  33.9 0.6 multiply_add_fusion
  34.5 0.7 compare_and_fusion
  35.2 17.9 %all-to-all-done = bf16[16,2,9,2048]{3,1,2,0:T(2,128)(2,1)} async-done(((bf16[16,2,9,2048]{3,1,2,0:T(2,128)(2,1)}), bf16[16,2,9,2048]{3,1,2,0:T(2,128)(2,1)}, u32[]{:S(2)}, u32[]{:S(2)}) %all-to-all-start) | async-done | bytes 1179680 | tf_op jit(solution)/shard_map/all_to_all | solution.py:17
  53.1 3.3 %copy.59 = bf16[16,2,9,2048]{3,2,1,0:T(8,128)(2,1)} copy(bf16[16,2,9,2048]{3,1,2,0:T(2,128)(2,1)} %all-to-all-done) | data formatting | bytes 2359296 | tf_op jit(solution)/shard_map/all_to_all | solution.py:17
  56.3 2.6 %reshape.121 = bf16[288,2048]{1,0:T(8,128)(2,1)} reshape(bf16[16,2,9,2048]{3,2,1,0:T(8,128)(2,1)} %copy.59) | data formatting | bytes 2359296 | tf_op jit(solution)/shard_map/reshape | solution.py:60
  59.0 4.9 %gather_fusion = bf16[256,2048]{1,0:T(8,128)(2,1)} fusion(bf16[288,2048]{1,0:T(8,128)(2,1)} %reshape.121, s32[1024]{0:T(1024)} %pad_clamp_fusion), kind=kCustom, calls=%fused_computation | custom fusion | bytes 2098176 | tf_op jit(solution)/shard_map/jit(_take)/gather | solution.py:64
  63.9 3.6 %multiply_reduce_fusion = bf16[2,16,2048]{2,1,0:T(8,128)(2,1)} fusion(f32[2,16,8]{2,1,0:T(8,128)S(1)} %copy.56, pred[2,16,8]{2,1,0:T(8,128)(4,1)S(1)} %copy-done.2, bf16[256,2048]{1,0:T(8,128)(2,1)} %gather_fusion), kind=kLoop, calls=%fused_computation.10 | loop fusion | flops 2031616 | bytes 1180928 | tf_op jit(solution)/shard_map/reduce_sum | solution.py:68
  67.5 3.4 %all-to-all-start.1 = ((bf16[2,16,2048]{2,1,0:T(8,128)(2,1)}), bf16[2,16,2048]{2,1,0:T(8,128)(2,1)S(1)}, u32[]{:S(2)}, u32[]{:S(2)}) async-start(bf16[2,16,2048]{2,1,0:T(8,128)(2,1)} %multiply_reduce_fusion), calls=%async_computation.1 | async-start | bytes 262144 | tf_op jit(solution)/shard_map/all_to_all | solution.py:69
  70.9 1.2 fusion.5
  72.1 2.2 %copy.63 = bf16[144,2,2048]{2,1,0:T(2,128)(2,1)} copy(bf16[144,2,2048]{2,0,1:T(8,128)(2,1)S(1)} %fusion.5) | data formatting | bytes 2359296 | tf_op jit(solution)/shard_map/convert_element_type | solution.py:51
  74.3 0.3 all-to-all-done.1
  74.6 5.7 %all-to-all-start.3 = ((bf16[16,9,2,2048]{3,2,1,0:T(2,128)(2,1)}), bf16[16,9,2,2048]{3,2,1,0:T(2,128)(2,1)}, u32[]{:S(2)}, u32[]{:S(2)}) async-start(bf16[16,9,2,2048]{3,2,1,0:T(2,128)(2,1)} %bitcast.58), calls=%async_computation.3 | async-start | bytes 2359296 | tf_op jit(solution)/shard_map/all_to_all | solution.py:17
  80.2 0.1 copy.60
  80.4 0.7 copy.70
  81.1 27.0 %all-to-all-done.3 = bf16[16,9,2,2048]{3,2,1,0:T(2,128)(2,1)} async-done(((bf16[16,9,2,2048]{3,2,1,0:T(2,128)(2,1)}), bf16[16,9,2,2048]{3,2,1,0:T(2,128)(2,1)}, u32[]{:S(2)}, u32[]{:S(2)}) %all-to-all-start.3) | async-done | bytes 1179680 | tf_op jit(solution)/shard_map/all_to_all | solution.py:17
  108.1 6.0 %convolution_bitcast_fusion = f32[1,768,2048]{1,2,0:T(8,128)} fusion(bf16[16,9,2,2048]{3,2,1,0:T(2,128)(2,1)} %all-to-all-done.3, bf16[2,1,16,9,768]{4,2,3,1,0:T(8,128)(2,1)} %copy-done.1), kind=kOutput, calls=%fused_computation.1 | convolution fusion | flops 905969664 | bytes 7913472 | tf_op jit(solution)/shard_map/rsjf,sjrd->fd/dot_general | solution.py:58
  114.1 6.6 %copy.66 = f32[1,768,2048]{2,1,0:T(8,128)} copy(f32[1,768,2048]{1,2,0:T(8,128)} %convolution_bitcast_fusion) | data formatting | bytes 12582912
  (19 shorter events, 0.3 us)
Async XLA Ops:
  0.6 13.9 %copy-start = (bf16[1,768,2048]{2,1,0:T(8,128)(2,1)S(1)}, bf16[1,768,2048]{2,1,0:T(8,128)(2,1)}, u32[]{:S(2)}) copy-start(bf16[1,768,2048]{2,1,0:T(8,128)(2,1)} %param.8) | copy-start | bytes 9437188
  2.4 15.5 %all-to-all-start.2 = ((bf16[16,2,2048]{2,0,1:T(8,128)(2,1)}), bf16[16,2,2048]{2,0,1:T(8,128)(2,1)S(1)}, u32[]{:S(2)}, u32[]{:S(2)}) async-start(bf16[16,2,2048]{2,0,1:T(8,128)(2,1)} %bitcast.57), calls=%async_computation.2 | async-start | bytes 262144 | tf_op jit(solution)/shard_map/all_to_all | solution.py:37
  13.8 0.8 copy-start.1
  15.6 9.6 %copy-start.4 = (s32[16,8]{0,1:T(8,128)S(1)}, s32[16,8]{0,1:T(8,128)}, u32[]{:S(2)}) copy-start(s32[16,8]{0,1:T(8,128)} %param.5) | copy-start | bytes 1540
  15.7 13.2 %copy-start.3 = (f32[16,8]{0,1:T(8,128)S(1)}, f32[16,8]{0,1:T(8,128)}, u32[]{:S(2)}) copy-start(f32[16,8]{0,1:T(8,128)} %param.6) | copy-start | bytes 1540
  17.9 35.2 %all-to-all-start = ((bf16[16,2,9,2048]{3,1,2,0:T(2,128)(2,1)}), bf16[16,2,9,2048]{3,1,2,0:T(2,128)(2,1)}, u32[]{:S(2)}, u32[]{:S(2)}) async-start(bf16[16,2,9,2048]{3,1,2,0:T(2,128)(2,1)} %copy.58), calls=%async_computation | async-start | bytes 2359296 | tf_op jit(solution)/shard_map/all_to_all | solution.py:17
  58.9 4.9 %copy-start.2 = (pred[2,16,8]{2,1,0:T(8,128)(4,1)S(1)}, pred[2,16,8]{2,1,0:T(8,128)(4,1)}, u32[]{:S(2)}) copy-start(pred[2,16,8]{2,1,0:T(8,128)(4,1)} %compare_and_fusion) | copy-start | bytes 772
  67.5 7.1 %all-to-all-start.1 = ((bf16[2,16,2048]{2,1,0:T(8,128)(2,1)}), bf16[2,16,2048]{2,1,0:T(8,128)(2,1)S(1)}, u32[]{:S(2)}, u32[]{:S(2)}) async-start(bf16[2,16,2048]{2,1,0:T(8,128)(2,1)} %multiply_reduce_fusion), calls=%async_computation.1 | async-start | bytes 262144 | tf_op jit(solution)/shard_map/all_to_all | solution.py:69
  74.6 33.5 %all-to-all-start.3 = ((bf16[16,9,2,2048]{3,2,1,0:T(2,128)(2,1)}), bf16[16,9,2,2048]{3,2,1,0:T(2,128)(2,1)}, u32[]{:S(2)}, u32[]{:S(2)}) async-start(bf16[16,9,2,2048]{3,2,1,0:T(2,128)(2,1)} %bitcast.58), calls=%async_computation.3 | async-start | bytes 2359296 | tf_op jit(solution)/shard_map/all_to_all | solution.py:17
where the time goes:
time: 121 us
  waiting for transfers between devices  45.2 us (37%)
  local copies, waits for them, and re-layouts  26.2 us (22%)
  starting transfers between devices  19.7 us (16%)
  blocking collectives  14.7 us (12%)
  matrix products  8.26 us (7%)
  other arithmetic  5.81 us (5%)
    all_to_all x2, waiting for transfers between devices, expert_move(): lax.all_to_all(buffer, ('ctx', 'tp'), split_axis=0, concat_axis=0, tiled=...  44.9 us
    all_to_all x2, starting transfers between devices, expert_move(): lax.all_to_all(buffer, ('ctx', 'tp'), split_axis=0, concat_axis=0, tiled=...  13 us
    unnamed x12, local copies, waits for them, and re-layouts  8.06 us
    all_gather x1, blocking collectives, body(): piece = lax.all_gather(hidden_rows, 'dp', axis=0, tiled=True)  8.01 us
    dot_general x1, matrix products, body(): jnp.einsum('rsjf,sjrd->fd', piece, grad_rows, preferred_element_type=jnp....  5.96 us
    gather x1, local copies, waits for them, and re-layouts, body(): jnp.take(returned, position, axis=0).astype(jnp.float32)  4.9 us
    reduce_sum x1, other arithmetic, body(): jnp.sum(all_gates[:, :, :, None] * picked, axis=2).astype(jnp.bfloat16)  3.65 us
    all_gather x1, blocking collectives, body(): lax.all_gather(routed_experts.astype(jnp.float32), 'dp', axis=0, tiled=True)  3.51 us
  transfers between devices with their start and end apart: 4, of which 3 were waited for; matrix products, arithmetic and copies ran while one was open for 9% of the time, Pallas kernels for 0%

commit v1 on v0

--- a/solution.py
+++ b/solution.py
@@ -1,6 +1,11 @@
+import functools
+
 import jax
 import jax.numpy as jnp
+import numpy as np
 from jax import lax
+from jax.experimental import pallas as pl
+from jax.experimental.pallas import tpu as pltpu
 from jax.sharding import PartitionSpec as P
 
 
@@ -70,6 +75,211 @@
     return (combined, gradient[None])
 
 
+MESH = pl.DeviceIdType.MESH
+
+
+def gate_parts(gates):
+    high = lax.reduce_precision(gates, 8, 7)
+    middle = lax.reduce_precision(gates - high, 8, 7)
+    return high, middle, gates - high - middle
+
+
+def fused_kernel(
+    sizes, table_ref, grad_ref, hidden_ref, weight_ref, base_ref, lower_ref,
+    combined_ref, tokens_ref, scaled_ref,
+    cut, rows, hidden, gate_col, part, core_out, core_in, y_out, y_in, z_out, z_in, last, halves,
+    dp_send, dp_recv, z_send, z_recv, y_send, y_recv, c_send, c_recv,
+    rc_send, rc_recv, ry_send, ry_recv, rz_send, rz_recv, rd_send, rd_recv,
+):
+    tok, topk, depth, lanes, ff, width, step = sizes
+    d, z, t = lax.axis_index("dp"), lax.axis_index("ctx"), lax.axis_index("tp")
+    core = lax.rem(t, 2)
+    y = lax.div(t, 2)
+    other = {"dp": 1 - d}
+    y_peer = (1 - y) * 2 + core
+    c_peer = y * 2 + 1 - core
+    per = depth * 2 * tok
+    block = 2 * tok
+
+    def at_z(k):
+        return lax.rem(z + k, depth)
+
+    def back(k):
+        return lax.rem(z - k + depth, depth)
+
+    def move(src, dst, send, recv, to):
+        return pltpu.make_async_remote_copy(
+            src_ref=src, dst_ref=dst, send_sem=send, recv_sem=recv,
+            device_id=to, device_id_type=MESH)
+
+    barrier = pltpu.get_barrier_semaphore()
+    peers = [other, {"tp": y_peer}, {"tp": c_peer}] + [{"ctx": at_z(k)} for k in range(1, depth)]
+    for peer in peers:
+        pl.semaphore_signal(barrier, inc=1, device_id=peer, device_id_type=MESH)
+    for half in range(2):
+        cut[half, :, :width] = grad_ref[:, half * width:(half + 1) * width]
+        cut[half, :, width:] = table_ref[...]
+    rows[t, z, d] = cut[d]
+    hidden[d] = hidden_ref[...]
+    pl.semaphore_wait(barrier, len(peers))
+
+    swap = move(cut.at[1 - d], rows.at[t, z, d], dp_send.at[0], dp_recv.at[0], other)
+    swap.start()
+    share = move(hidden_ref, hidden.at[d], dp_send.at[1], dp_recv.at[1], other)
+    share.start()
+    swap.wait_recv()
+    z_moves, y_moves, c_moves = [], [], []
+    for k in range(1, depth):
+        z_moves.append(move(rows.at[t, z], rows.at[t, z], z_send.at[k], z_recv.at[k], {"ctx": at_z(k)}))
+        z_moves[-1].start()
+    for k in range(depth):
+        own = rows.at[t, back(k)]
+        if k:
+            z_moves[k - 1].wait_recv()
+        y_moves.append(move(own, own, y_send.at[k], y_recv.at[k], {"tp": y_peer}))
+        y_moves[-1].start()
+        c_moves.append(move(own, own, c_send.at[k], c_recv.at[k], {"tp": c_peer}))
+        c_moves[-1].start()
+    for k in range(depth):
+        y_moves[k].wait_recv()
+        own = rows.at[y_peer, back(k)]
+        c_moves.append(move(own, own, c_send.at[depth + k], c_recv.at[depth + k], {"tp": c_peer}))
+        c_moves[-1].start()
+    for copy in c_moves:
+        copy.wait_recv()
+    share.wait_recv()
+
+    expert = (z * lanes + t).astype(jnp.float32)
+    tokens = rows.shape[0] * per
+    table = rows[:, :, :, :, width:].reshape(tokens, 128).astype(jnp.float32)
+    lane = lax.broadcasted_iota(jnp.int32, (tokens, 128), 1)
+    named = jnp.where(jnp.logical_and(lane < topk, table == expert), 1.0, 0.0)
+    spread = pltpu.roll(named, topk, 1) + pltpu.roll(named, 2 * topk, 1) + pltpu.roll(named, 3 * topk, 1)
+    gate_col[...] = jnp.sum(spread * table, axis=1, keepdims=True)
+    before = jnp.dot(lower_ref[...], named.astype(jnp.bfloat16), preferred_element_type=jnp.float32)
+    rank = jnp.sum(before, axis=1, keepdims=True)
+    slot = jnp.where(jnp.sum(named, axis=1, keepdims=True) > 0.5, base_ref[...] + rank, -1.0)
+    slots = 2 * hidden.shape[1]
+    place = lax.broadcasted_iota(jnp.int32, (tokens, slots), 1).astype(jnp.float32)
+    placer = jnp.where(place == slot, 1.0, 0.0).astype(jnp.bfloat16)
+    picked = jnp.dot(placer, hidden[...].reshape(slots, ff), preferred_element_type=jnp.float32)
+    tokens_ref[...] = picked.astype(jnp.bfloat16).reshape(tokens_ref.shape)
+
+    def forward(group, out):
+        left = tokens_ref[group]
+        gate = gate_col[pl.ds(pl.multiple_of(group * per, per), per), :]
+
+        @pl.loop(0, width // step)
+        def _(c):
+            columns = pl.ds(pl.multiple_of(c * step, step), step)
+            made = jnp.dot(left, weight_ref[:, columns], preferred_element_type=jnp.float32)
+            made = made.astype(jnp.bfloat16).astype(jnp.float32) * gate
+            out[:, columns] = made.astype(out.dtype)
+
+    core_moves = []
+    for i, side in enumerate((1 - y, y)):
+        forward(side * 2 + 1 - core, core_out.at[i])
+        core_moves.append(move(core_out.at[i], core_in.at[i], rc_send.at[i], rc_recv.at[i], {"tp": c_peer}))
+        core_moves[-1].start()
+    for i, side in enumerate((1 - y, y)):
+        forward(side * 2 + core, part.at[i])
+    back_moves = []
+    core_moves[0].wait_recv()
+    for k in range(depth):
+        where = at_z(k + 1)
+        span = pl.ds(pl.multiple_of(where * block, block), block)
+        y_out[k] = (part[0, span] + core_in[0, span].astype(jnp.float32)).astype(jnp.bfloat16)
+        back_moves.append(move(y_out.at[k], y_in.at[k], ry_send.at[k], ry_recv.at[k], {"tp": y_peer}))
+        back_moves[-1].start()
+
+    core_moves[1].wait_recv()
+
+    @pl.loop(0, tokens // block)
+    def _(c):
+        span = pl.ds(pl.multiple_of(c * block, block), block)
+        gate = gate_col[span, :]
+        grads = rows[lax.div(c, depth), lax.rem(c, depth)][:, :, :width].reshape(block, width)
+        scaled_ref[span, :] = (gate * grads.astype(jnp.float32)).astype(jnp.bfloat16)
+
+    out_moves = []
+    for k in range(depth):
+        where = at_z(k + 1)
+        span = pl.ds(pl.multiple_of(where * block, block), block)
+        back_moves[k].wait_recv()
+        total = part[1, span] + core_in[1, span].astype(jnp.float32) + y_in[k].astype(jnp.float32)
+        if k < depth - 1:
+            z_out[k] = total.astype(jnp.bfloat16)
+            out_moves.append(move(z_out.at[k], z_in.at[k], rz_send.at[k], rz_recv.at[k], {"ctx": where}))
+            out_moves[-1].start()
+    for k in range(depth - 1):
+        out_moves[k].wait_recv()
+        total = total + z_in[k].astype(jnp.float32)
+    for r in range(2):
+        last[r] = total[r * tok:(r + 1) * tok].astype(jnp.bfloat16)
+    halves[d] = last[d]
+    finish = move(last.at[1 - d], halves.at[d], rd_send, rd_recv, other)
+    finish.start()
+    finish.wait_recv()
+    for half in range(2):
+        combined_ref[:, half * width:(half + 1) * width] = halves[half]
+    for copy in [swap, share, finish] + z_moves + y_moves + c_moves + core_moves + back_moves + out_moves:
+        copy.wait_send()
+
+
+def fused_body(routed_experts, route_gates, expert_hidden, down_weight, output_grad):
+    depth, lanes = lax.axis_size("ctx"), lax.axis_size("tp")
+    tok, topk = routed_experts.shape
+    capacity, ff = expert_hidden.shape[3:]
+    slots = depth * lanes * capacity
+    width = output_grad.shape[1] // 2
+    tokens = 2 * depth * lanes * tok
+    per = tokens // lanes
+    step = 512 if width % 512 == 0 else width
+    table = jnp.concatenate([routed_experts.astype(jnp.float32), *gate_parts(route_gates)], axis=1)
+    table = jnp.pad(table, ((0, 0), (0, 128 - 4 * topk))).astype(jnp.bfloat16)
+    index = np.arange(tokens)
+    place = index // tok
+    source = place % 2 * (depth * lanes) + place // 2 % depth * lanes + place // (2 * depth)
+    base = jnp.asarray((source * capacity)[:, None], jnp.float32)
+    lower = jnp.asarray((place[:, None] == place[None]) & (index[None] < index[:, None]), jnp.bfloat16)
+    vmem = pl.BlockSpec(memory_space=pltpu.VMEM)
+    wide, half = width + 128, jnp.bfloat16
+    dma = pltpu.SemaphoreType.DMA
+    combined, picked, scaled = pl.pallas_call(
+        functools.partial(fused_kernel, (tok, topk, depth, lanes, ff, width, step)),
+        out_shape=(
+            jax.ShapeDtypeStruct(output_grad.shape, half),
+            jax.ShapeDtypeStruct((lanes, per, ff), half),
+            jax.ShapeDtypeStruct((tokens, width), half),
+        ),
+        in_specs=[vmem] * 6,
+        out_specs=[vmem] * 3,
+        scratch_shapes=[
+            pltpu.VMEM((2, tok, wide), half),
+            pltpu.VMEM((lanes, depth, 2, tok, wide), half),
+            pltpu.VMEM((2, slots, ff), half),
+            pltpu.VMEM((tokens, 1), jnp.float32),
+            pltpu.VMEM((2, per, width), jnp.float32),
+            pltpu.VMEM((2, per, width), half),
+            pltpu.VMEM((2, per, width), half),
+            pltpu.VMEM((depth, 2 * tok, width), half),
+            pltpu.VMEM((depth, 2 * tok, width), half),
+            pltpu.VMEM((depth, 2 * tok, width), half),
+            pltpu.VMEM((depth, 2 * tok, width), half),
+            pltpu.VMEM((2, tok, width), half),
+            pltpu.VMEM((2, tok, width), half),
+            dma((2,)), dma((2,)), dma((depth,)), dma((depth,)), dma((depth,)), dma((depth,)),
+            dma((2 * depth,)), dma((2 * depth,)),
+            dma((2,)), dma((2,)), dma((depth,)), dma((depth,)), dma((depth,)), dma((depth,)), dma, dma,
+        ],
+        compiler_params=pltpu.CompilerParams(
+            collective_id=0, has_side_effects=True, vmem_limit_bytes=40 * 1024 * 1024),
+    )(table, output_grad, expert_hidden.reshape(slots, ff), down_weight[0], base, lower)
+    gradient = lax.dot_general(
+        picked.reshape(tokens, ff), scaled, (((0,), (0,)), ((), ())), preferred_element_type=jnp.float32)
+    return combined, gradient[None]
+
+
 def solution(mesh):
     in_specs = (
         P(("dp", "ctx", "tp"), None),
@@ -79,4 +289,5 @@
         P(("dp", "ctx", "tp"), None),
     )
     out_specs = (P(("dp", "ctx", "tp"), None), P(("ctx", "tp"), None, "dp"))
-    return jax.shard_map(body, mesh=mesh, in_specs=in_specs, out_specs=out_specs, check_vma=False)
+    pairs = mesh.shape["dp"] == 2 and mesh.shape["tp"] == 4
+    return jax.shard_map(fused_body if pairs else body, mesh=mesh, in_specs=in_specs, out_specs=out_specs, check_vma=False)

time: 121 us -> 67.8 us (0.56)
  the two profiles are of different devices: /device:TPU:13 before, /device:TPU:0 now
where the time goes in v1:
time: 67.8 us; the launch traced here: 67.1 us
  Pallas kernels  52.9 us (78%)
  local copies, waits for them, and re-layouts  7.47 us (11%)
  matrix products  4.54 us (7%)
  other arithmetic  1.47 us (2%)
    pallas_call x1, Pallas kernels, fused_body(): pl.pallas_call(functools.partial(fused_kernel, (tok, topk, depth, lanes,...  52.9 us
    unnamed x11, local copies, waits for them, and re-layouts  7.21 us
    dot_general x1, matrix products, fused_body(): lax.dot_general(picked.reshape(tokens, ff), scaled, (((0,), (0,)), ((), (...  4.54 us

profile of v1, /device:TPU:0, one launch (start us, length us, event | category | flops | bytes accessed | tf_op | source)
XLA Modules:
  0.0 67.1 jit_solution(14434440416313463847)
XLA Ops:
  0.6 0.7 %convert_element_type.6 = bf16[16,8]{0,1:T(8,128)(2,1)S(1)} convert(s32[16,8]{0,1:T(8,128)} %param.7) | non-fusion elementwise | flops 128 | bytes 768 | tf_op jit(solution)/shard_map/convert_element_type | solution.py:238
  1.3 0.1 copy.17
  1.4 0.7 %reduce_precision.6 = f32[16,8]{0,1:T(8,128)S(1)} reduce-precision(f32[16,8]{0,1:T(8,128)} %param.8), exponent_bits=8, mantissa_bits=7 | non-fusion elementwise | flops 128 | bytes 1024 | tf_op jit(solution)/shard_map/reduce_precision | solution.py:82
  2.1 0.1 copy.18
  2.2 0.8 %copy.19 = f32[16,8]{1,0:T(8,128)S(1)} copy(f32[16,8]{0,1:T(8,128)} %param.8) | data formatting | bytes 1024 | tf_op args[1]
  2.9 0.1 fusion.7.table_ref
  3.0 1.0 %copy.21 = bf16[1,1,16,9,768]{4,3,2,1,0:T(8,128)(2,1)S(1)} copy(bf16[1,1,16,9,768]{4,2,3,1,0:T(8,128)(2,1)} %param.9) | data formatting | bytes 442368 | tf_op args[2]
  4.0 0.1 reshape.10.hidden_ref
  4.2 0.0 copy-start
  4.2 1.9 %copy-done = bf16[1,768,2048]{2,1,0:T(8,128)(2,1)S(1)} copy-done((bf16[1,768,2048]{2,1,0:T(8,128)(2,1)S(1)}, bf16[1,768,2048]{2,1,0:T(8,128)(2,1)}, u32[]{:S(2)}) %copy-start) | copy-done | bytes 3145752
  6.0 0.0 copy-start.1
  6.0 1.0 %copy-done.1 = bf16[512,512]{1,0:T(8,128)(2,1)S(1)} copy-done((bf16[512,512]{1,0:T(8,128)(2,1)S(1)}, bf16[512,512]{1,0:T(8,128)(2,1)}, u32[]{:S(2)}) %copy-start.1) | copy-done | bytes 524312
  7.1 0.0 copy-start.2
  7.1 0.9 %copy-done.2 = f32[512,1]{1,0:T(8,128)S(1)} copy-done((f32[512,1]{1,0:T(8,128)S(1)}, f32[512,1]{1,0:T(8,128)}, u32[]{:S(2)}) %copy-start.2) | copy-done | bytes 2072
  8.0 0.0 copy-start.3
  8.0 0.9 %copy-done.3 = bf16[16,4096]{1,0:T(8,128)(2,1)S(1)} copy-done((bf16[16,4096]{1,0:T(8,128)(2,1)S(1)}, bf16[16,4096]{1,0:T(8,128)(2,1)}, u32[]{:S(2)}) %copy-start.3) | copy-done | bytes 131096
  8.9 52.9 %shard_map.86 = (bf16[16,4096]{1,0:T(8,128)(2,1)S(1)}, bf16[4,128,768]{2,1,0:T(8,128)(2,1)S(1)}, bf16[512,2048]{1,0:T(8,128)(2,1)S(1)}) custom-call(bf16[16,128]{1,0:T(8,128)(2,1)S(1)} %fusion.7.table_ref, bf16[16,4096]{1,0:T(8,128)(2,1)S(1)} %copy-done.3, bf16[144,768]{1,0:T(8,128)(2,1)S(1)} %reshape.10.hidden_ref, bf16[768,2048]{1,0:T(8,128)(2,1)S(1)} %bitcast.6, ...), custom_call_target="tpu_custom_call" | custom-call | tf_op jit(solution)/shard_map/pallas_call | solution.py:248
  61.9 4.5 %convolution_bitcast_fusion = f32[1,768,2048]{2,1,0:T(8,128)} fusion(bf16[512,768]{1,0:T(8,128)(2,1)S(1)} %bitcast.7, bf16[512,2048]{1,0:T(8,128)(2,1)S(1)} %get-tuple-element.7), kind=kOutput, calls=%fused_computation | convolution fusion | flops 1610612736 | bytes 9175040 | tf_op jit(solution)/shard_map/dot_general | solution.py:278
  66.4 0.7 copy.23
  (1 shorter events, 0.0 us)
Async XLA Ops:
  4.2 1.9 %copy-start = (bf16[1,768,2048]{2,1,0:T(8,128)(2,1)S(1)}, bf16[1,768,2048]{2,1,0:T(8,128)(2,1)}, u32[]{:S(2)}) copy-start(bf16[1,768,2048]{2,1,0:T(8,128)(2,1)} %param.10) | copy-start | bytes 9437188
  6.0 1.0 %copy-start.1 = (bf16[512,512]{1,0:T(8,128)(2,1)S(1)}, bf16[512,512]{1,0:T(8,128)(2,1)}, u32[]{:S(2)}) copy-start(bf16[512,512]{1,0:T(8,128)(2,1)} %constant.9.clone.lower_ref) | copy-start | bytes 1572868
  7.1 0.9 %copy-start.2 = (f32[512,1]{1,0:T(8,128)S(1)}, f32[512,1]{1,0:T(8,128)}, u32[]{:S(2)}) copy-start(f32[512,1]{1,0:T(8,128)} %constant.8.clone.base_ref) | copy-start | bytes 6148
  8.0 0.9 %copy-start.3 = (bf16[16,4096]{1,0:T(8,128)(2,1)S(1)}, bf16[16,4096]{1,0:T(8,128)(2,1)}, u32[]{:S(2)}) copy-start(bf16[16,4096]{1,0:T(8,128)(2,1)} %grad_ref.1) | copy-start | bytes 393220

commit v2 on v1

v2 whole, which is shorter than its diff:
```python
import functools

import jax
import jax.numpy as jnp
from jax import lax
from jax.experimental import pallas as pl
from jax.experimental.pallas import tpu as pltpu
from jax.sharding import PartitionSpec as P


def slot_ranks(flat_experts):
    count = flat_experts.shape[-1]
    same = flat_experts[..., :, None] == flat_experts[..., None, :]
    before = lax.broadcasted_iota(jnp.int32, (count, count), 1) < lax.broadcasted_iota(
        jnp.int32, (count, count), 0
    )
    return jnp.sum(jnp.logical_and(same, before), axis=-1)


def expert_move(buffer):
    return lax.all_to_all(buffer, ("ctx", "tp"), split_axis=0, concat_axis=0, tiled=True)


def body(routed_experts, route_gates, expert_hidden, down_weight, output_grad):
    replicas = lax.axis_size("dp")
    sources = lax.axis_size("ctx") * lax.axis_size("tp")
    tok_own, topk = routed_experts.shape
    routes = tok_own * topk
    capacity = expert_hidden.shape[3]
    width = output_grad.shape[1]
    column_part = width // replicas
    hidden_rows = expert_hidden[0]
    weight = down_weight[0]
    slot_count = sources * capacity
    expert_table, gate_table = (
        lax.all_gather(routed_experts.astype(jnp.float32), "dp", axis=0, tiled=True),
        lax.all_gather(route_gates, "dp", axis=0, tiled=True),
    )
    all_experts = expert_table.astype(jnp.int32).reshape(replicas, routes)
    all_gates = gate_table.reshape(replicas, tok_own, topk)
    grad_columns = lax.all_to_all(
        output_grad, "dp", split_axis=1, concat_axis=0, tiled=True
    ).reshape(replicas, tok_own, 1, column_part)
    ranks = slot_ranks(all_experts)
    target = all_experts * capacity + ranks
    placer = (
        lax.broadcasted_iota(jnp.int32, (1, slot_count, routes), 1) == target[:, None, :]
    ).astype(jnp.bfloat16)
    scaled = (
        (all_gates[:, :, :, None] * grad_columns.astype(jnp.float32))
        .reshape(replicas, routes, column_part)
        .astype(jnp.bfloat16)
    )
    outgoing = jnp.einsum("rpq,rqd->prd", placer, scaled, preferred_element_type=jnp.float32)
    outgoing = outgoing.astype(jnp.bfloat16).reshape(sources, capacity, replicas, column_part)
    grad_rows = expert_move(outgoing)
    piece = lax.all_gather(hidden_rows, "dp", axis=0, tiled=True)
    produced = jnp.einsum(
        "rsjf,fd->srjd", piece, weight, preferred_element_type=jnp.float32
    ).astype(jnp.bfloat16)
    outputs = produced
    gradient = jnp.einsum("rsjf,sjrd->fd", piece, grad_rows, preferred_element_type=jnp.float32)
    outputs, gradient = (outputs, gradient)
    returned = expert_move(outputs).reshape(sources * replicas * capacity, column_part)
    replica_index = lax.broadcasted_iota(jnp.int32, (replicas, routes), 0)
    position = all_experts * (replicas * capacity) + replica_index * capacity + ranks
    picked = (
        jnp.take(returned, position, axis=0)
        .astype(jnp.float32)
        .reshape(replicas, tok_own, topk, column_part)
    )
    partial_rows = jnp.sum(all_gates[:, :, :, None] * picked, axis=2).astype(jnp.bfloat16)
    combined = lax.all_to_all(partial_rows, "dp", split_axis=0, concat_axis=2, tiled=True)[0]
    return (combined, gradient[None])


MESH = pl.DeviceIdType.MESH


def fused_kernel(
    sizes, routes_ref, gates_ref, grad_ref, hidden_ref, weight_ref,
    combined_ref, tokens_ref, scaled_ref,
    stack, tables, rows, hidden, weight, base, lower, gate_col,
    part, core_out, core_in, y_out, y_in, z_out, z_in, last, halves,
    local_sem, dp_send, dp_recv, tz_send, tz_recv, ty_send, ty_recv, tc_send, tc_recv,
    z_send, z_recv, y_send, y_recv, c_send, c_recv,
    rc_send, rc_recv, ry_send, ry_recv, rz_send, rz_recv,
):
    tok, topk, depth, lanes, ff, width, step = sizes
    d, z, t = lax.axis_index("dp"), lax.axis_index("ctx"), lax.axis_index("tp")
    core = lax.rem(t, 2)
    y = lax.div(t, 2)
    other = {"dp": 1 - d}
    y_peer = {"tp": (1 - y) * 2 + core}
    c_peer = {"tp": y * 2 + 1 - core}
    here, across = core * 2 + y, core * 2 + 1 - y
    per = depth * 2 * tok
    block = 2 * tok
    tokens = lanes * per

    def at_z(k):
        return lax.rem(z + k, depth)

    def back(k):
        return lax.rem(z - k + depth, depth)

    def send(src, dst, send_sem, recv_sem, to):
        copy = pltpu.make_async_remote_copy(
            src_ref=src, dst_ref=dst, send_sem=send_sem, recv_sem=recv_sem,
            device_id=to, device_id_type=MESH)
        copy.start()
        return copy

    def columns_of(half):
        return grad_ref.at[:, pl.ds(pl.multiple_of(half * width, 128), width)]

    barrier = pltpu.get_barrier_semaphore()
    peers = [other, y_peer, c_peer] + [{"ctx": at_z(k)} for k in range(1, depth)]
    for peer in peers:
        pl.semaphore_signal(barrier, inc=1, device_id=peer, device_id_type=MESH)
    local = []
    for i, (src, dst) in enumerate((
        (columns_of(d), rows.at[here, z, d]), (hidden_ref, hidden.at[d]),
        (weight_ref, weight),
    )):
        local.append(pltpu.make_async_copy(src, dst, local_sem.at[i]))
        local[-1].start()
    gates = gates_ref[...]
    high = gates.astype(jnp.bfloat16).astype(jnp.float32)
    middle = (gates - high).astype(jnp.bfloat16).astype(jnp.float32)
    stack[0:topk] = routes_ref[...].astype(jnp.float32)
    stack[topk:2 * topk] = high
    stack[2 * topk:3 * topk] = middle
    stack[3 * topk:] = gates - high - middle
    spread_rows = lax.broadcasted_iota(jnp.int32, (4 * topk, 128), 0)
    spread_lanes = lax.broadcasted_iota(jnp.int32, (4 * topk, 128), 1)
    spreader = jnp.where(spread_rows == spread_lanes, 1.0, 0.0).astype(jnp.bfloat16)
    tables[here, z, d] = lax.dot_general(
        stack[...].astype(jnp.bfloat16), spreader, (((0,), (0,)), ((), ())),
        preferred_element_type=jnp.float32).astype(jnp.bfloat16)
    pl.semaphore_wait(barrier, len(peers))

    own = tables.at[here, z, d]
    sent = [send(own, own, dp_send.at[0], dp_recv.at[0], other)]
    sent.append(send(columns_of(1 - d), rows.at[here, z, d], dp_send.at[1], dp_recv.at[1], other))
    sent.append(send(hidden_ref, hidden.at[d], dp_send.at[2], dp_recv.at[2], other))

    def spread_z(buffer, sends, recvs):
        own = buffer.at[here, z]
        return [send(own, own, sends.at[k], recvs.at[k], {"ctx": at_z(k)}) for k in range(1, depth)]

    def hand(buffer, group, k, slot, sends, recvs, to):
        own = buffer.at[group, back(k)]
        return send(own, own, sends.at[slot], recvs.at[slot], to)

    sources = depth * lanes
    for q in range(lanes):
        for k in range(2 * depth):
            origin = k % 2 * (sources * (hidden.shape[1] // sources)) + k // 2 * lanes + q % 2 * 2 + q // 2
            start = q * per + k * tok
            base[start:start + tok] = jnp.full((tok, 1), float(origin), jnp.float32)
    lower_rows = lax.broadcasted_iota(jnp.int32, (tok, tokens), 0)
    lower_lanes = lax.broadcasted_iota(jnp.int32, (tok, tokens), 1)

    @pl.loop(0, tokens // tok)
    def _(c):
        earlier = jnp.logical_and(lower_lanes >= c * tok, lower_lanes < lower_rows + c * tok)
        lower[pl.ds(pl.multiple_of(c * tok, tok), tok), :] = jnp.where(earlier, 1.0, 0.0).astype(jnp.bfloat16)

    sent[0].wait_recv()
    tz = spread_z(tables, tz_send, tz_recv)
    ty, tc, yy, cc = [], [], [], []
    ty.append(hand(tables, here, 0, 0, ty_send, ty_recv, y_peer))
    tc.append(hand(tables, here, 0, 0, tc_send, tc_recv, c_peer))
    local[0].wait()
    sent[1].wait_recv()
    zz = spread_z(rows, z_send, z_recv)
    yy.append(hand(rows, here, 0, 0, y_send, y_recv, y_peer))
    cc.append(hand(rows, here, 0, 0, c_send, c_recv, c_peer))
    for k in range(1, depth):
        tz[k - 1].wait_recv()
        ty.append(hand(tables, here, k, k, ty_send, ty_recv, y_peer))
        tc.append(hand(tables, here, k, k, tc_send, tc_recv, c_peer))
    for k in range(depth):
        ty[k].wait_recv()
        tc.append(hand(tables, across, k, depth + k, tc_send, tc_recv, c_peer))
    for copy in tc:
        copy.wait_recv()

    expert = (z * lanes + t).astype(jnp.float32)
    table = tables[...].reshape(tokens, 128).astype(jnp.float32)
    lane = lax.broadcasted_iota(jnp.int32, (tokens, 128), 1)
    named = jnp.where(jnp.logical_and(lane < topk, table == expert), 1.0, 0.0)
    spread = pltpu.roll(named, topk, 1) + pltpu.roll(named, 2 * topk, 1) + pltpu.roll(named, 3 * topk, 1)
    gate_col[...] = jnp.sum(spread * table, axis=1, keepdims=True)
    before = jnp.dot(lower[...], named.astype(jnp.bfloat16), preferred_element_type=jnp.float32)
    rank = jnp.sum(before, axis=1, keepdims=True)
    used = jnp.sum(named, axis=1, keepdims=True) > 0.5
    slot = jnp.where(used, base[...] + rank * (depth * lanes), -1.0)
    slots = 2 * hidden.shape[1]
    place = lax.broadcasted_iota(jnp.int32, (tokens, slots), 1).astype(jnp.float32)
    placer = jnp.where(place == slot, 1.0, 0.0).astype(jnp.bfloat16)
    local[1].wait()
    sent[2].wait_recv()
    picked = jnp.dot(placer, hidden[...].reshape(slots, ff), preferred_element_type=jnp.float32)
    tokens_ref[...] = picked.astype(jnp.bfloat16).reshape(tokens_ref.shape)
    local[2].wait()

    def forward(side, out):
        left = tokens_ref[side]
        gate = gate_col[pl.ds(pl.multiple_of(side * 2 * per, per), 2 * per), :]

        @pl.loop(0, width // step)
        def _(c):
            columns = pl.ds(pl.multiple_of(c * step, step), step)
            made = jnp.dot(left, weight[:, columns], preferred_element_type=jnp.float32)
            made = made.astype(jnp.bfloat16).astype(jnp.float32) * gate
            for half in range(2):
                out[half, :, columns] = made[half * per:(half + 1) * per].astype(out.dtype)

    forward(1 - core, core_out)
    core_moves = []
    for i, side in enumerate((1 - y, y)):
        core_moves.append(send(core_out.at[side], core_in.at[side], rc_send.at[i], rc_recv.at[i], c_peer))
    for k in range(1, depth):
        zz[k - 1].wait_recv()
        yy.append(hand(rows, here, k, k, y_send, y_recv, y_peer))
        cc.append(hand(rows, here, k, k, c_send, c_recv, c_peer))
    forward(core, part)
    core_moves[0].wait_recv()
    back_moves = []
    for k in range(depth):
        span = pl.ds(pl.multiple_of(at_z(k + 1) * block, block), block)
        y_out[k] = (part[1 - y, span] + core_in[1 - y, span].astype(jnp.float32)).astype(jnp.bfloat16)
        back_moves.append(send(y_out.at[k], y_in.at[k], ry_send.at[k], ry_recv.at[k], y_peer))
    for k in range(depth):
        yy[k].wait_recv()
        cc.append(hand(rows, across, k, depth + k, c_send, c_recv, c_peer))
    core_moves[1].wait_recv()
    out_moves = []
    for k in range(depth):
        where = at_z(k + 1)
        span = pl.ds(pl.multiple_of(where * block, block), block)
        back_moves[k].wait_recv()
        total = part[y, span] + core_in[y, span].astype(jnp.float32) + y_in[k].astype(jnp.float32)
        if k < depth - 1:
            z_out[k] = total.astype(jnp.bfloat16)
            out_moves.append(send(z_out.at[k], z_in.at[k], rz_send.at[k], rz_recv.at[k], {"ctx": where}))
    for copy in cc:
        copy.wait_recv()

    @pl.loop(0, tokens // block)
    def _(c):
        span = pl.ds(pl.multiple_of(c * block, block), block)
        gate = gate_col[span, :]
        grads = rows[lax.div(c, depth), lax.rem(c, depth)].reshape(block, width)
        scaled_ref[span, :] = (gate * grads.astype(jnp.float32)).astype(jnp.bfloat16)

    for k in range(depth - 1):
        out_moves[k].wait_recv()
        total = total + z_in[k].astype(jnp.float32)
    for r in range(2):
        last[r] = total[r * tok:(r + 1) * tok].astype(jnp.bfloat16)
    finish = send(last.at[1 - d], halves.at[d], dp_send.at[3], dp_recv.at[3], other)
    halves[d] = last[d]
    finish.wait_recv()
    for half in range(2):
        combined_ref[:, half * width:(half + 1) * width] = halves[half]
    for copy in sent + [finish] + tz + ty + tc + zz + yy + cc + core_moves + back_moves + out_moves:
        copy.wait_send()


def fused_body(routed_experts, route_gates, expert_hidden, down_weight, output_grad):
    depth, lanes = lax.axis_size("ctx"), lax.axis_size("tp")
    tok, topk = routed_experts.shape
    capacity, ff = expert_hidden.shape[3:]
    sources = depth * lanes
    slots = sources * capacity
    width = output_grad.shape[1] // 2
    tokens = 2 * depth * lanes * tok
    per = tokens // lanes
    step = 512 if width % 512 == 0 else width
    vmem = pl.BlockSpec(memory_space=pltpu.VMEM)
    hbm = pl.BlockSpec(memory_space=pltpu.HBM)
    half = jnp.bfloat16
    dma = pltpu.SemaphoreType.DMA
    four, eight = dma((depth,)), dma((2 * depth,))
    combined, picked, scaled = pl.pallas_call(
        functools.partial(fused_kernel, (tok, topk, depth, lanes, ff, width, step)),
        out_shape=(
            jax.ShapeDtypeStruct(output_grad.shape, half),
            jax.ShapeDtypeStruct((2, 2 * per, ff), half),
            jax.ShapeDtypeStruct((tokens, width), half),
        ),
        in_specs=[vmem] * 2 + [hbm] * 3,
        out_specs=[vmem] * 3,
        scratch_shapes=[
            pltpu.VMEM((4 * topk, tok), jnp.float32),
            pltpu.VMEM((lanes, depth, 2, tok, 128), half),
            pltpu.VMEM((lanes, depth, 2, tok, width), half),
            pltpu.VMEM((2, slots, ff), half),
            pltpu.VMEM(down_weight.shape[1:], half),
            pltpu.VMEM((tokens, 1), jnp.float32),
            pltpu.VMEM((tokens, tokens), half),
            pltpu.VMEM((tokens, 1), jnp.float32),
            pltpu.VMEM((2, per, width), jnp.float32),
            pltpu.VMEM((2, per, width), half),
            pltpu.VMEM((2, per, width), half),
            pltpu.VMEM((depth, 2 * tok, width), half),
            pltpu.VMEM((depth, 2 * tok, width), half),
            pltpu.VMEM((depth, 2 * tok, width), half),
            pltpu.VMEM((depth, 2 * tok, width), half),
            pltpu.VMEM((2, tok, width), half),
            pltpu.VMEM((2, tok, width), half),
            dma((3,)), dma((4,)), dma((4,)), four, four, four, four, eight, eight,
            four, four, four, four, eight, eight,
            dma((2,)), dma((2,)), four, four, four, four,
        ],
        compiler_params=pltpu.CompilerParams(
            collective_id=0, has_side_effects=True, vmem_limit_bytes=58 * 1024 * 1024),
    )(
        routed_experts.T, route_gates.T, output_grad,
        expert_hidden[0, 0].transpose(1, 0, 2).reshape(slots, ff), down_weight[0])
    gradient = lax.dot_general(
        picked.reshape(tokens, ff), scaled, (((0,), (0,)), ((), ())), preferred_element_type=jnp.float32)
    return combined, gradient[None]


def solution(mesh):
    in_specs = (
        P(("dp", "ctx", "tp"), None),
        P(("dp", "ctx", "tp"), None),
        P(("ctx", "tp"), "dp", None, None, None),
        P(("ctx", "tp"), None, "dp"),
        P(("dp", "ctx", "tp"), None),
    )
    out_specs = (P(("dp", "ctx", "tp"), None), P(("ctx", "tp"), None, "dp"))
    pairs = mesh.shape["dp"] == 2 and mesh.shape["tp"] == 4
    return jax.shard_map(fused_body if pairs else body, mesh=mesh, in_specs=in_specs, out_specs=out_specs, check_vma=False)
```

time: 67.8 us -> 59 us (0.87)
  local copies, waits for them, and re-layouts: 7.47 us -> 0.66 us
  Pallas kernels: 52.9 us -> 51 us
  matrix products: 4.54 us -> 6.4 us
  other arithmetic: 1.47 us -> 0 us
    unnamed x11 -> x3, local copies, waits for them, and re-layouts: 7.21 us -> 0.66 us
    pallas_call x1, Pallas kernels: 52.9 us -> 51 us  [fused_body(): pl.pallas_call(functools.partial(fused_kernel, (tok, topk, depth, lanes,...]
    dot_general x1, matrix products: 4.54 us -> 6.4 us  [fused_body(): lax.dot_general(picked.reshape(tokens, ff), scaled, (((0,), (0,)), ((), (...]
    convert_element_type x1 -> x0, other arithmetic: 0.69 us -> none  [fused_body(): routed_experts.astype(jnp.float32)]
    reduce_precision x1 -> x0, other arithmetic: 0.69 us -> none  [gate_parts(): high = lax.reduce_precision(gates, 8, 7)]
where the time goes in v2:
time: 59 us; the launch traced here: 58.8 us
  Pallas kernels  51 us (86%)
  matrix products  6.4 us (11%)
  local copies, waits for them, and re-layouts  0.66 us (1%)
  between operations  0.65 us (1%)
    pallas_call x1, Pallas kernels, fused_body(): pl.pallas_call(functools.partial(fused_kernel, (tok, topk, depth, lanes,...  51 us
    dot_general x1, matrix products, fused_body(): lax.dot_general(picked.reshape(tokens, ff), scaled, (((0,), (0,)), ((), (...  6.4 us

profile of v2, /device:TPU:0, one launch (start us, length us, event | category | flops | bytes accessed | tf_op | source)
XLA Modules:
  0.0 58.8 jit_solution(13253730543385549605)
XLA Ops:
  0.6 51.0 %shard_map.68 = (bf16[16,4096]{1,0:T(8,128)(2,1)}, bf16[2,256,768]{2,1,0:T(8,128)(2,1)}, bf16[512,2048]{1,0:T(8,128)(2,1)}) custom-call(s32[8,16]{1,0:T(8,128)} %bitcast.16, f32[8,16]{1,0:T(8,128)} %bitcast.17, bf16[16,4096]{1,0:T(8,128)(2,1)} %grad_ref.1, bf16[144,768]{1,0:T(8,128)(2,1)} %bitcast.15, bf16[768,2048]{1,0:T(8,128)(2,1)} %bitcast.13), custom_call_target="tpu_custom_call" | custom-call | tf_op jit(solution)/shard_map/pallas_call | solution.py:288
  51.7 0.0 copy-start
  51.7 6.4 %convolution_bitcast_fusion = f32[1,768,2048]{2,1,0:T(8,128)} fusion(bf16[512,768]{1,0:T(8,128)(2,1)} %bitcast.14, bf16[512,2048]{1,0:T(8,128)(2,1)} %get-tuple-element.7), kind=kOutput, calls=%fused_computation | convolution fusion | flops 1610612736 | bytes 9175040 | tf_op jit(solution)/shard_map/dot_general | solution.py:324
  58.1 0.0 copy-done
  58.1 0.7 %copy.8 = bf16[16,4096]{1,0:T(8,128)(2,1)} copy(bf16[16,4096]{1,0:T(8,128)(2,1)S(1)} %copy-done) | data formatting | bytes 262144
Async XLA Ops:
  51.7 6.4 %copy-start = (bf16[16,4096]{1,0:T(8,128)(2,1)S(1)}, bf16[16,4096]{1,0:T(8,128)(2,1)}, u32[]{:S(2)}) copy-start(bf16[16,4096]{1,0:T(8,128)(2,1)} %get-tuple-element.10) | copy-start | bytes 393220

commit v3 on v2

--- a/solution.py
+++ b/solution.py
@@ -167,16 +167,65 @@
         earlier = jnp.logical_and(lower_lanes >= c * tok, lower_lanes < lower_rows + c * tok)
         lower[pl.ds(pl.multiple_of(c * tok, tok), tok), :] = jnp.where(earlier, 1.0, 0.0).astype(jnp.bfloat16)
 
+    def line(where, k, leftward, to):
+        own = rows.at[here, where]
+        slot = depth + k if leftward else k
+        return pltpu.make_async_remote_copy(
+            src_ref=own, dst_ref=own, send_sem=z_send.at[slot], recv_sem=z_recv.at[slot],
+            device_id={"ctx": to}, device_id_type=MESH)
+
+    def hands(group, where, slot, far):
+        own = rows.at[group, where]
+        mine = 2 * depth + slot if far else slot
+        to_core = pltpu.make_async_remote_copy(
+            src_ref=own, dst_ref=own, send_sem=c_send.at[mine], recv_sem=c_recv.at[mine],
+            device_id=c_peer, device_id_type=MESH)
+        if far:
+            return [to_core]
+        return [pltpu.make_async_remote_copy(
+            src_ref=own, dst_ref=own, send_sem=y_send.at[slot], recv_sem=y_recv.at[slot],
+            device_id=y_peer, device_id_type=MESH), to_core]
+
+    def onward(where, k, slot):
+        moves = []
+        if slot < depth:
+            moves.append((z < depth - 1, line(where, k + 1, False, at_z(1))))
+        if slot >= depth or k == 0:
+            moves.append((z > 0, line(where, k + 1, True, back(1))))
+        return moves if k + 1 < depth else []
+
+    def pass_on(where, k, *slots):
+        for ready, copy in onward(where, k, 0) if k == 0 else onward(where, k, slots[0]):
+            pl.when(ready)(copy.start)
+        for copy in hands(here, where, 0 if k == 0 else slots[0], False):
+            copy.start()
+
+    def arrivals(k):
+        return ((z >= k, back(k), k), (z + k < depth, at_z(k), depth + k))
+
+    def relay(k):
+        for valid, where, slot in arrivals(k):
+            @pl.when(valid)
+            def _(where=where, slot=slot):
+                line(where, k, slot >= depth, at_z(1)).wait_recv()
+                pass_on(where, k, slot)
+
+    def each_block(act):
+        act(z, 0, 0)
+        for k in range(1, depth):
+            for valid, where, slot in arrivals(k):
+                @pl.when(valid)
+                def _(where=where, slot=slot, k=k):
+                    act(where, k, slot)
+
     sent[0].wait_recv()
     tz = spread_z(tables, tz_send, tz_recv)
-    ty, tc, yy, cc = [], [], [], []
+    ty, tc = [], []
     ty.append(hand(tables, here, 0, 0, ty_send, ty_recv, y_peer))
     tc.append(hand(tables, here, 0, 0, tc_send, tc_recv, c_peer))
     local[0].wait()
     sent[1].wait_recv()
-    zz = spread_z(rows, z_send, z_recv)
-    yy.append(hand(rows, here, 0, 0, y_send, y_recv, y_peer))
-    cc.append(hand(rows, here, 0, 0, c_send, c_recv, c_peer))
+    pass_on(z, 0)
     for k in range(1, depth):
         tz[k - 1].wait_recv()
         ty.append(hand(tables, here, k, k, ty_send, ty_recv, y_peer))
@@ -184,6 +233,7 @@
     for k in range(depth):
         ty[k].wait_recv()
         tc.append(hand(tables, across, k, depth + k, tc_send, tc_recv, c_peer))
+    relay(1)
     for copy in tc:
         copy.wait_recv()
 
@@ -204,6 +254,7 @@
     sent[2].wait_recv()
     picked = jnp.dot(placer, hidden[...].reshape(slots, ff), preferred_element_type=jnp.float32)
     tokens_ref[...] = picked.astype(jnp.bfloat16).reshape(tokens_ref.shape)
+    relay(2)
     local[2].wait()
 
     def forward(side, out):
@@ -222,10 +273,8 @@
     core_moves = []
     for i, side in enumerate((1 - y, y)):
         core_moves.append(send(core_out.at[side], core_in.at[side], rc_send.at[i], rc_recv.at[i], c_peer))
-    for k in range(1, depth):
-        zz[k - 1].wait_recv()
-        yy.append(hand(rows, here, k, k, y_send, y_recv, y_peer))
-        cc.append(hand(rows, here, k, k, c_send, c_recv, c_peer))
+    for k in range(3, depth):
+        relay(k)
     forward(core, part)
     core_moves[0].wait_recv()
     back_moves = []
@@ -233,9 +282,11 @@
         span = pl.ds(pl.multiple_of(at_z(k + 1) * block, block), block)
         y_out[k] = (part[1 - y, span] + core_in[1 - y, span].astype(jnp.float32)).astype(jnp.bfloat16)
         back_moves.append(send(y_out.at[k], y_in.at[k], ry_send.at[k], ry_recv.at[k], y_peer))
-    for k in range(depth):
-        yy[k].wait_recv()
-        cc.append(hand(rows, across, k, depth + k, c_send, c_recv, c_peer))
+    def cross(where, k, slot):
+        hands(here, where, slot, False)[0].wait_recv()
+        hands(across, where, slot, True)[0].start()
+
+    each_block(cross)
     core_moves[1].wait_recv()
     out_moves = []
     for k in range(depth):
@@ -246,8 +297,11 @@
         if k < depth - 1:
             z_out[k] = total.astype(jnp.bfloat16)
             out_moves.append(send(z_out.at[k], z_in.at[k], rz_send.at[k], rz_recv.at[k], {"ctx": where}))
-    for copy in cc:
-        copy.wait_recv()
+    def landed(where, k, slot):
+        for far in (False, True):
+            hands(here, where, slot, far)[-1].wait_recv()
+
+    each_block(landed)
 
     @pl.loop(0, tokens // block)
     def _(c):
@@ -266,8 +320,16 @@
     finish.wait_recv()
     for half in range(2):
         combined_ref[:, half * width:(half + 1) * width] = halves[half]
-    for copy in sent + [finish] + tz + ty + tc + zz + yy + cc + core_moves + back_moves + out_moves:
+    for copy in sent + [finish] + tz + ty + tc + core_moves + back_moves + out_moves:
         copy.wait_send()
+
+    def left(where, k, slot):
+        for ready, copy in onward(where, k, slot):
+            pl.when(ready)(copy.wait_send)
+        for copy in hands(here, where, slot, False) + hands(across, where, slot, True):
+            copy.wait_send()
+
+    each_block(left)
 
 
 def fused_body(routed_experts, route_gates, expert_hidden, down_weight, output_grad):
@@ -313,7 +375,7 @@
             pltpu.VMEM((2, tok, width), half),
             pltpu.VMEM((2, tok, width), half),
             dma((3,)), dma((4,)), dma((4,)), four, four, four, four, eight, eight,
-            four, four, four, four, eight, eight,
+            eight, eight, eight, eight, dma((4 * depth,)), dma((4 * depth,)),
             dma((2,)), dma((2,)), four, four, four, four,
         ],
         compiler_params=pltpu.CompilerParams(

time: 59 us -> 54 us (0.915)
  Pallas kernels: 51 us -> 46.1 us
    pallas_call x1, Pallas kernels: 51 us -> 46.1 us  [fused_body(): pl.pallas_call(functools.partial(fused_kernel, (tok, topk, depth, lanes,...]
where the time goes in v3:
time: 54 us; the launch traced here: 53.8 us
  Pallas kernels  46.1 us (85%)
  matrix products  6.41 us (12%)
  local copies, waits for them, and re-layouts  0.66 us (1%)
  between operations  0.65 us (1%)
    pallas_call x1, Pallas kernels, fused_body(): pl.pallas_call(functools.partial(fused_kernel, (tok, topk, depth, lanes,...  46.1 us
    dot_general x1, matrix products, fused_body(): lax.dot_general(picked.reshape(tokens, ff), scaled, (((0,), (0,)), ((), (...  6.41 us

profile of v3, /device:TPU:0, one launch (start us, length us, event | category | flops | bytes accessed | tf_op | source)
XLA Modules:
  0.0 53.8 jit_solution(4271244196012623564)
XLA Ops:
  0.6 46.1 %shard_map.68 = (bf16[16,4096]{1,0:T(8,128)(2,1)}, bf16[2,256,768]{2,1,0:T(8,128)(2,1)}, bf16[512,2048]{1,0:T(8,128)(2,1)}) custom-call(s32[8,16]{1,0:T(8,128)} %bitcast.16, f32[8,16]{1,0:T(8,128)} %bitcast.17, bf16[16,4096]{1,0:T(8,128)(2,1)} %grad_ref.1, bf16[144,768]{1,0:T(8,128)(2,1)} %bitcast.15, bf16[768,2048]{1,0:T(8,128)(2,1)} %bitcast.13), custom_call_target="tpu_custom_call" | custom-call | tf_op jit(solution)/shard_map/pallas_call | solution.py:350
  46.7 0.0 copy-start
  46.8 6.4 %convolution_bitcast_fusion = f32[1,768,2048]{2,1,0:T(8,128)} fusion(bf16[512,768]{1,0:T(8,128)(2,1)} %bitcast.14, bf16[512,2048]{1,0:T(8,128)(2,1)} %get-tuple-element.7), kind=kOutput, calls=%fused_computation | convolution fusion | flops 1610612736 | bytes 9175040 | tf_op jit(solution)/shard_map/dot_general | solution.py:386
  53.2 0.0 copy-done
  53.2 0.7 %copy.8 = bf16[16,4096]{1,0:T(8,128)(2,1)} copy(bf16[16,4096]{1,0:T(8,128)(2,1)S(1)} %copy-done) | data formatting | bytes 262144
Async XLA Ops:
  46.7 6.4 %copy-start = (bf16[16,4096]{1,0:T(8,128)(2,1)S(1)}, bf16[16,4096]{1,0:T(8,128)(2,1)}, u32[]{:S(2)}) copy-start(bf16[16,4096]{1,0:T(8,128)(2,1)} %get-tuple-element.10) | copy-start | bytes 393220

commit v4 on v3

--- a/solution.py
+++ b/solution.py
@@ -79,7 +79,8 @@
 
 def fused_kernel(
     sizes, routes_ref, gates_ref, grad_ref, hidden_ref, weight_ref,
-    combined_ref, tokens_ref, scaled_ref,
+    combined_ref, tokens_out, scaled_out,
+    tokens_ref, scaled_ref,
     stack, tables, rows, hidden, weight, base, lower, gate_col,
     part, core_out, core_in, y_out, y_in, z_out, z_in, last, halves,
     local_sem, dp_send, dp_recv, tz_send, tz_recv, ty_send, ty_recv, tc_send, tc_recv,
@@ -254,6 +255,8 @@
     sent[2].wait_recv()
     picked = jnp.dot(placer, hidden[...].reshape(slots, ff), preferred_element_type=jnp.float32)
     tokens_ref[...] = picked.astype(jnp.bfloat16).reshape(tokens_ref.shape)
+    keep_tokens = pltpu.make_async_copy(tokens_ref, tokens_out, local_sem.at[3])
+    keep_tokens.start()
     relay(2)
     local[2].wait()
 
@@ -273,9 +276,9 @@
     core_moves = []
     for i, side in enumerate((1 - y, y)):
         core_moves.append(send(core_out.at[side], core_in.at[side], rc_send.at[i], rc_recv.at[i], c_peer))
+    forward(core, part)
     for k in range(3, depth):
         relay(k)
-    forward(core, part)
     core_moves[0].wait_recv()
     back_moves = []
     for k in range(depth):
@@ -310,6 +313,8 @@
         grads = rows[lax.div(c, depth), lax.rem(c, depth)].reshape(block, width)
         scaled_ref[span, :] = (gate * grads.astype(jnp.float32)).astype(jnp.bfloat16)
 
+    keep_scaled = pltpu.make_async_copy(scaled_ref, scaled_out, local_sem.at[4])
+    keep_scaled.start()
     for k in range(depth - 1):
         out_moves[k].wait_recv()
         total = total + z_in[k].astype(jnp.float32)
@@ -330,6 +335,8 @@
             copy.wait_send()
 
     each_block(left)
+    keep_tokens.wait()
+    keep_scaled.wait()
 
 
 def fused_body(routed_experts, route_gates, expert_hidden, down_weight, output_grad):
@@ -355,8 +362,10 @@
             jax.ShapeDtypeStruct((tokens, width), half),
         ),
         in_specs=[vmem] * 2 + [hbm] * 3,
-        out_specs=[vmem] * 3,
+        out_specs=[vmem, hbm, hbm],
         scratch_shapes=[
+            pltpu.VMEM((2, 2 * per, ff), half),
+            pltpu.VMEM((tokens, width), half),
             pltpu.VMEM((4 * topk, tok), jnp.float32),
             pltpu.VMEM((lanes, depth, 2, tok, 128), half),
             pltpu.VMEM((lanes, depth, 2, tok, width), half),
@@ -374,7 +383,7 @@
             pltpu.VMEM((depth, 2 * tok, width), half),
             pltpu.VMEM((2, tok, width), half),
             pltpu.VMEM((2, tok, width), half),
-            dma((3,)), dma((4,)), dma((4,)), four, four, four, four, eight, eight,
+            dma((5,)), dma((4,)), dma((4,)), four, four, four, four, eight, eight,
             eight, eight, eight, eight, dma((4 * depth,)), dma((4 * depth,)),
             dma((2,)), dma((2,)), four, four, four, four,
         ],

time: 54 us -> 53 us (0.981)
  Pallas kernels: 46.1 us -> 45.1 us
    pallas_call x1, Pallas kernels: 46.1 us -> 45.1 us  [fused_body(): pl.pallas_call(functools.partial(fused_kernel, (tok, topk, depth, lanes,...]
where the time goes in v4:
time: 53 us; the launch traced here: 52.8 us
  Pallas kernels  45.1 us (85%)
  matrix products  6.4 us (12%)
  local copies, waits for them, and re-layouts  0.66 us (1%)
  between operations  0.65 us (1%)
    pallas_call x1, Pallas kernels, fused_body(): pl.pallas_call(functools.partial(fused_kernel, (tok, topk, depth, lanes,...  45.1 us
    dot_general x1, matrix products, fused_body(): lax.dot_general(picked.reshape(tokens, ff), scaled, (((0,), (0,)), ((), (...  6.4 us

profile of v4, /device:TPU:0, one launch (start us, length us, event | category | flops | bytes accessed | tf_op | source)
XLA Modules:
  0.0 52.8 jit_solution(11062230968494575139)
XLA Ops:
  0.6 45.1 %shard_map.68 = (bf16[16,4096]{1,0:T(8,128)(2,1)}, bf16[2,256,768]{2,1,0:T(8,128)(2,1)}, bf16[512,2048]{1,0:T(8,128)(2,1)}) custom-call(s32[8,16]{1,0:T(8,128)} %bitcast.16, f32[8,16]{1,0:T(8,128)} %bitcast.17, bf16[16,4096]{1,0:T(8,128)(2,1)} %grad_ref.1, bf16[144,768]{1,0:T(8,128)(2,1)} %bitcast.15, bf16[768,2048]{1,0:T(8,128)(2,1)} %bitcast.13), custom_call_target="tpu_custom_call" | custom-call | tf_op jit(solution)/shard_map/pallas_call | solution.py:357
  45.7 0.0 copy-start
  45.8 6.4 %convolution_bitcast_fusion = f32[1,768,2048]{2,1,0:T(8,128)} fusion(bf16[512,768]{1,0:T(8,128)(2,1)} %bitcast.14, bf16[512,2048]{1,0:T(8,128)(2,1)} %get-tuple-element.7), kind=kOutput, calls=%fused_computation | convolution fusion | flops 1610612736 | bytes 9175040 | tf_op jit(solution)/shard_map/dot_general | solution.py:395
  52.2 0.0 copy-done
  52.2 0.7 %copy.8 = bf16[16,4096]{1,0:T(8,128)(2,1)} copy(bf16[16,4096]{1,0:T(8,128)(2,1)S(1)} %copy-done) | data formatting | bytes 262144
Async XLA Ops:
  45.7 6.4 %copy-start = (bf16[16,4096]{1,0:T(8,128)(2,1)S(1)}, bf16[16,4096]{1,0:T(8,128)(2,1)}, u32[]{:S(2)}) copy-start(bf16[16,4096]{1,0:T(8,128)(2,1)} %get-tuple-element.10) | copy-start | bytes 393220

commit v5 on v4

--- a/solution.py
+++ b/solution.py
@@ -277,14 +277,15 @@
     for i, side in enumerate((1 - y, y)):
         core_moves.append(send(core_out.at[side], core_in.at[side], rc_send.at[i], rc_recv.at[i], c_peer))
     forward(core, part)
-    for k in range(3, depth):
-        relay(k)
     core_moves[0].wait_recv()
     back_moves = []
     for k in range(depth):
         span = pl.ds(pl.multiple_of(at_z(k + 1) * block, block), block)
         y_out[k] = (part[1 - y, span] + core_in[1 - y, span].astype(jnp.float32)).astype(jnp.bfloat16)
         back_moves.append(send(y_out.at[k], y_in.at[k], ry_send.at[k], ry_recv.at[k], y_peer))
+    for k in range(3, depth):
+        relay(k)
+
     def cross(where, k, slot):
         hands(here, where, slot, False)[0].wait_recv()
         hands(across, where, slot, True)[0].start()

time: 53 us -> 58.7 us (1.11)
  the two profiles are of different devices: /device:TPU:0 before, /device:TPU:24 now
where the time goes in v5:
time: 58.7 us; the launch traced here: 58.5 us
  Pallas kernels  50.8 us (87%)
  matrix products  6.41 us (11%)
  local copies, waits for them, and re-layouts  0.66 us (1%)
  between operations  0.65 us (1%)
    pallas_call x1, Pallas kernels, fused_body(): pl.pallas_call(functools.partial(fused_kernel, (tok, topk, depth, lanes,...  50.8 us
    dot_general x1, matrix products, fused_body(): lax.dot_general(picked.reshape(tokens, ff), scaled, (((0,), (0,)), ((), (...  6.41 us

profile of v5, /device:TPU:24, one launch (start us, length us, event | category | flops | bytes accessed | tf_op | source)
XLA Modules:
  0.0 58.5 jit_solution(65525230349748119)
XLA Ops:
  0.6 50.8 %shard_map.68 = (bf16[16,4096]{1,0:T(8,128)(2,1)}, bf16[2,256,768]{2,1,0:T(8,128)(2,1)}, bf16[512,2048]{1,0:T(8,128)(2,1)}) custom-call(s32[8,16]{1,0:T(8,128)} %bitcast.16, f32[8,16]{1,0:T(8,128)} %bitcast.17, bf16[16,4096]{1,0:T(8,128)(2,1)} %grad_ref.1, bf16[144,768]{1,0:T(8,128)(2,1)} %bitcast.15, bf16[768,2048]{1,0:T(8,128)(2,1)} %bitcast.13), custom_call_target="tpu_custom_call" | custom-call | tf_op jit(solution)/shard_map/pallas_call | solution.py:358
  51.4 0.0 copy-start
  51.4 6.4 %convolution_bitcast_fusion = f32[1,768,2048]{2,1,0:T(8,128)} fusion(bf16[512,768]{1,0:T(8,128)(2,1)} %bitcast.14, bf16[512,2048]{1,0:T(8,128)(2,1)} %get-tuple-element.7), kind=kOutput, calls=%fused_computation | convolution fusion | flops 1610612736 | bytes 9175040 | tf_op jit(solution)/shard_map/dot_general | solution.py:396
  57.8 0.0 copy-done
  57.8 0.7 %copy.8 = bf16[16,4096]{1,0:T(8,128)(2,1)} copy(bf16[16,4096]{1,0:T(8,128)(2,1)S(1)} %copy-done) | data formatting | bytes 262144
Async XLA Ops:
  51.4 6.4 %copy-start = (bf16[16,4096]{1,0:T(8,128)(2,1)S(1)}, bf16[16,4096]{1,0:T(8,128)(2,1)}, u32[]{:S(2)}) copy-start(bf16[16,4096]{1,0:T(8,128)(2,1)} %get-tuple-element.10) | copy-start | bytes 393220
